TPU v7x, 32 devices: a whole 2x2x4 slice. The times are simulated.
32 devices in a mesh: scene: 2 (over x), tok: 16 (over z, y, core).
Axes of the slice: x: 2, y: 2, z: 4, core: 2. Of those that a mesh axis runs over, the one named last changes fastest.
Arguments:
- tokens: bfloat16 [16384, 768], P(('scene', 'tok')), parts along dimension 0, may hold values from -6 to 6
- qkv_weight: bfloat16 [768, 2304], replicated, may hold values from -0.21875 to 0.21875
- w_gate: float32 [4, 192, 384], replicated, may hold values from -0.4375 to 0.4375
- w_up: float32 [4, 192, 384], replicated, may hold values from -0.4375 to 0.4375
- w_down: float32 [4, 384, 192], replicated, may hold values from -0.3125 to 0.3125
- view_kind: int32 [32], P('scene'), parts along dimension 0, may hold values from 0 to 1, as said below
Outputs:
- mixed: bfloat16 [16384, 768], P(('scene', 'tok')), parts along dimension 0
There are 2 independent parts, one for each index of `scene`. A program takes and returns all parts, laid end to end along the dimension named above; an argument that names none is the same for every part. Nothing has to cross between parts.
Inputs may be any that keep to these rules, and one draw needn't show every extreme that they name: `view_kind`: exactly 12 of the 16 views are input views.
All inputs are finite; a program needn't handle non-finite values.
Results may differ from a plain program's by a relative error of at most 0.03.
Values may be sent and summed in bfloat16 or wider, within the bound.
No kernel may reach another device: no remote copies, remote signals or barrier semaphores. Data moves between devices by JAX's collectives and lax.ppermute only.
A program may use at most 64 MiB of HBM per device.

v0:
```python
import jax
import jax.numpy as jnp
from jax import lax
from jax.sharding import PartitionSpec as P

VIEWS = 16
NS_STEPS = 5
coef_a = 3.4445
coef_b = -4.775
coef_c = 2.0315
step_size = 0.8


def newton(start):
    iterate = start
    for step in range(NS_STEPS):
        gram = jnp.einsum(
            "mik,mjk->mij", iterate, iterate, preferred_element_type=jnp.float32
        ).astype(jnp.bfloat16)
        square = jnp.einsum("mij,mjk->mik", gram, gram, preferred_element_type=jnp.float32)
        mixer = (coef_b * gram.astype(jnp.float32) + coef_c * square).astype(jnp.bfloat16)
        moved = jnp.einsum("mij,mjk->mik", mixer, iterate, preferred_element_type=jnp.float32)
        iterate = (coef_a * iterate.astype(jnp.float32) + moved).astype(jnp.bfloat16)
    return iterate


def shards(tokens, qkv_weight, w_gate, w_up, w_down, view_kind):
    rows, width = tokens.shape
    heads, head_dim, hidden_dim = w_gate.shape
    groups = lax.axis_size("tok")
    place = lax.axis_index("tok")
    view_rows = rows * groups // VIEWS
    owner = place * rows // view_rows
    flag = jnp.sum(jnp.where(jnp.arange(VIEWS, dtype=jnp.int32) == owner, view_kind, 0))
    proj = jnp.dot(tokens, qkv_weight, preferred_element_type=jnp.float32).astype(jnp.bfloat16)
    query = proj[:, :width].reshape(rows, heads, head_dim)
    keys = proj[:, width : 2 * width].reshape(rows, heads, head_dim)
    values = proj[:, 2 * width :].reshape(rows, heads, head_dim)
    masked = values * flag.astype(jnp.bfloat16)
    gate_b = w_gate.astype(jnp.bfloat16)
    up_b = w_up.astype(jnp.bfloat16)
    down_b = w_down.astype(jnp.bfloat16)
    gate = jnp.einsum("thd,hdf->thf", keys, gate_b, preferred_element_type=jnp.float32)
    upper = jnp.einsum("thd,hdf->thf", keys, up_b, preferred_element_type=jnp.float32)
    sig = jax.nn.sigmoid(gate)
    act = gate * sig
    hidden = (act * upper).astype(jnp.bfloat16)
    dhid = -jnp.einsum("the,hfe->thf", masked, down_b, preferred_element_type=jnp.float32)
    dgate = (dhid * upper * (sig * (1.0 + gate * (1.0 - sig)))).astype(jnp.bfloat16)
    dup = (dhid * act).astype(jnp.bfloat16)
    grad_gate = jnp.einsum("thd,thf->hdf", keys, dgate, preferred_element_type=jnp.float32)
    grad_up = jnp.einsum("thd,thf->hdf", keys, dup, preferred_element_type=jnp.float32)
    grad_down = -jnp.einsum("the,thf->hef", masked, hidden, preferred_element_type=jnp.float32)
    grads = jnp.concatenate([grad_gate, grad_up, grad_down], axis=0)
    total = lax.psum(grads, "tok")
    norms = jnp.sqrt(jnp.sum(total * total, axis=(1, 2)))
    start = (total / (norms + 1e-07)[:, None, None]).astype(jnp.bfloat16)
    ortho = newton(start)
    stacked = jnp.concatenate([w_gate, w_up, jnp.transpose(w_down, (0, 2, 1))], axis=0)
    fresh = (stacked - step_size * ortho.astype(jnp.float32)).astype(jnp.bfloat16)
    gate2 = jnp.einsum("thd,hdf->thf", query, fresh[:heads], preferred_element_type=jnp.float32)
    upper2 = jnp.einsum(
        "thd,hdf->thf", query, fresh[heads : 2 * heads], preferred_element_type=jnp.float32
    )
    hidden2 = (jax.nn.silu(gate2) * upper2).astype(jnp.bfloat16)
    result = jnp.einsum(
        "thf,hef->the", hidden2, fresh[2 * heads :], preferred_element_type=jnp.float32
    )
    return result.reshape(rows, width).astype(jnp.bfloat16)


def solution(mesh):
    placed = (P(("scene", "tok"), None), P(), P(), P(), P(), P("scene"))
    return jax.shard_map(
        shards, mesh=mesh, in_specs=placed, out_specs=P(("scene", "tok"), None), check_vma=False
    )
```

profile of v0, /device:TPU:0, one launch (start us, length us, event | category | flops | bytes accessed | tf_op | source)
XLA Modules:
  0.0 202.8 jit_solution(2150129931057547903)
XLA Ops:
  6.5 1.4 fusion.39
  8.6 3.1 %convolution_convert_fusion = bf16[512,2304]{1,0:T(8,128)(2,1)S(1)} fusion(bf16[512,768]{1,0:T(8,128)(2,1)} %param.6, bf16[768,2304]{1,0:T(8,128)(2,1)S(1)} %copy-done), kind=kOutput, calls=%fused_computation | convolution fusion | flops 1813118976 | bytes 6684672 | tf_op jit(solution)/shard_map/dot_general | solution.py:35
  11.8 1.5 fusion.53
  13.3 2.3 %copy.17 = bf16[512,768]{0,1:T(8,128)(2,1)} copy(bf16[512,768]{1,0:T(8,128)(2,1)} %get-tuple-element.6) | data formatting | bytes 1572864 | tf_op jit(solution)/shard_map/mul | solution.py:39
  15.6 2.3 %copy.16 = bf16[512,768]{0,1:T(8,128)(2,1)} copy(bf16[512,768]{1,0:T(8,128)(2,1)} %get-tuple-element.7) | data formatting | bytes 1572864 | tf_op jit(solution)/shard_map/slice | solution.py:37
  17.9 2.5 %fusion.33 = f32[4,512,384]{2,1,0:T(8,128)S(1)} fusion(bf16[512,4,192]{0,2,1:T(8,128)(2,1)} %bitcast.110, f32[4,192,384]{2,1,0:T(8,128)} %param.8), kind=kOutput, calls=%fused_computation.59 | convolution fusion | flops 302284800 | bytes 5111808 | tf_op jit(solution)/shard_map/thd,hdf->thf/dot_general | solution.py:43
  20.4 0.8 fusion.35
  21.9 0.8 fusion.37
  22.7 1.1 fusion.20
  23.9 1.9 fusion.18
  25.7 1.1 fusion.14
  26.8 2.1 %pad_maximum_fusion = f32[12,192,384]{2,1,0:T(8,128)} fusion(f32[4,192,384]{2,1,0:T(8,128)S(1)} %fusion.20, f32[4,192,384]{2,1,0:T(8,128)S(1)} %fusion.14, f32[4,192,384]{2,1,0:T(8,128)S(1)} %fusion.18), kind=kLoop, calls=%fused_computation.3 | loop fusion | flops 1769472 | bytes 7077888 | tf_op jit(solution)/shard_map/concatenate | solution.py:54
  28.9 2.3 %copy.18 = bf16[512,768]{0,1:T(8,128)(2,1)} copy(bf16[512,768]{1,0:T(8,128)(2,1)} %get-tuple-element.5) | data formatting | bytes 1572864 | tf_op jit(solution)/shard_map/slice | solution.py:36
  31.2 106.7 %all-reduce.2.cloned.1.call-done = f32[12,192,384]{2,1,0:T(8,128)} async-done(((f32[12,192,384]{2,1,0:T(8,128)}), f32[12,192,384]{2,1,0:T(8,128)}) %all-reduce.2.cloned.1.call-update) | async-done | bytes 3538960 | tf_op jit(solution)/shard_map/psum | solution.py:55
  138.0 2.5 %multiply_reduce_fusion = f32[12]{0:T(128)S(1)} fusion(f32[12,192,384]{2,1,0:T(8,128)} %all-reduce.2.cloned.1.call-done), kind=kLoop, calls=%fused_computation.10 | loop fusion | flops 1769460 | bytes 3538992 | tf_op jit(solution)/shard_map/reduce_sum | solution.py:56
  140.5 0.5 copy-done.2
  141.0 0.4 divide_convert_fusion
  141.5 1.2 copy-done.1
  142.7 1.8 convolution_convert_fusion.5
  144.5 5.5 %add_convert_fusion.4 = bf16[12,192,384]{2,1,0:T(8,128)(2,1)} fusion(bf16[12,192,384]{2,1,0:T(8,128)(2,1)} %copy-done.1, bf16[12,192,192]{2,1,0:T(8,128)(2,1)} %convolution_convert_fusion.5), kind=kOutput, calls=%fused_computation.8 | convolution fusion | flops 515358720 | bytes 4423680 | tf_op jit(solution)/shard_map/mij,mjk->mik/dot_general | solution.py:22
  150.0 3.8 %convolution_convert_fusion.4 = bf16[12,192,192]{2,1,0:T(8,128)(2,1)} fusion(bf16[12,192,384]{2,1,0:T(8,128)(2,1)} %add_convert_fusion.4), kind=kOutput, calls=%fused_computation.44 | convolution fusion | flops 340180992 | bytes 2654208 | tf_op jit(solution)/shard_map/mik,mjk->mij/dot_general | solution.py:17
  153.8 5.6 %add_convert_fusion.3 = bf16[12,192,384]{2,1,0:T(8,128)(2,1)} fusion(bf16[12,192,384]{2,1,0:T(8,128)(2,1)} %add_convert_fusion.4, bf16[12,192,192]{2,1,0:T(8,128)(2,1)} %convolution_convert_fusion.4), kind=kOutput, calls=%fused_computation.7 | convolution fusion | flops 515358720 | bytes 4423680 | tf_op jit(solution)/shard_map/mij,mjk->mik/dot_general | solution.py:22
  159.4 3.8 %convolution_convert_fusion.3 = bf16[12,192,192]{2,1,0:T(8,128)(2,1)} fusion(bf16[12,192,384]{2,1,0:T(8,128)(2,1)} %add_convert_fusion.3), kind=kOutput, calls=%fused_computation.43 | convolution fusion | flops 340180992 | bytes 2654208 | tf_op jit(solution)/shard_map/mik,mjk->mij/dot_general | solution.py:17
  163.2 5.5 %add_convert_fusion.2 = bf16[12,192,384]{2,1,0:T(8,128)(2,1)} fusion(bf16[12,192,384]{2,1,0:T(8,128)(2,1)} %add_convert_fusion.3, bf16[12,192,192]{2,1,0:T(8,128)(2,1)} %convolution_convert_fusion.3), kind=kOutput, calls=%fused_computation.6 | convolution fusion | flops 515358720 | bytes 4423680 | tf_op jit(solution)/shard_map/mij,mjk->mik/dot_general | solution.py:22
  168.7 3.8 %convolution_convert_fusion.2 = bf16[12,192,192]{2,1,0:T(8,128)(2,1)} fusion(bf16[12,192,384]{2,1,0:T(8,128)(2,1)} %add_convert_fusion.2), kind=kOutput, calls=%fused_computation.42 | convolution fusion | flops 340180992 | bytes 2654208 | tf_op jit(solution)/shard_map/mik,mjk->mij/dot_general | solution.py:17
  172.6 5.6 %add_convert_fusion.1 = bf16[12,192,384]{2,1,0:T(8,128)(2,1)} fusion(bf16[12,192,384]{2,1,0:T(8,128)(2,1)} %add_convert_fusion.2, bf16[12,192,192]{2,1,0:T(8,128)(2,1)} %convolution_convert_fusion.2), kind=kOutput, calls=%fused_computation.5 | convolution fusion | flops 515358720 | bytes 4423680 | tf_op jit(solution)/shard_map/mij,mjk->mik/dot_general | solution.py:22
  178.2 3.8 %convolution_convert_fusion.1 = bf16[12,192,192]{2,1,0:T(8,128)(2,1)} fusion(bf16[12,192,384]{2,1,0:T(8,128)(2,1)} %add_convert_fusion.1), kind=kOutput, calls=%fused_computation.41 | convolution fusion | flops 340180992 | bytes 2654208 | tf_op jit(solution)/shard_map/mik,mjk->mij/dot_general | solution.py:17
  182.0 6.7 %fusion = bf16[12,192,384]{2,1,0:T(8,128)(2,1)} fusion(f32[4,192,384]{2,1,0:T(8,128)} %bitcast.116, f32[4,192,384]{2,1,0:T(8,128)} %param.9, f32[4,192,384]{2,1,0:T(8,128)} %param.8, bf16[12,192,384]{2,1,0:T(8,128)(2,1)} %add_convert_fusion.1, bf16[12,192,192]{2,1,0:T(8,128)(2,1)} %convolution_convert_fusion.1), kind=kOutput, calls=%fused_computation.2 | convolution fusion | flops 520667136 | bytes 7962624 | tf_op jit(solution)/shard_map/mij,mjk->mik/dot_general | solution.py:22
  188.7 2.3 %fusion.54 = f32[4,384,512]{1,2,0:T(8,128)S(1)} fusion(bf16[12,192,384]{2,1,0:T(8,128)(2,1)} %fusion, bf16[512,4,192]{0,2,1:T(8,128)(2,1)} %bitcast.117), kind=kOutput, calls=%fused_computation.82 | convolution fusion | flops 301989888 | bytes 5701632 | tf_op jit(solution)/shard_map/thd,hdf->thf/dot_general | solution.py:61
  191.0 1.1 fusion.1
  192.1 1.6 convolution_convert_fusion.6
  193.7 2.3 %copy.20 = bf16[512,768]{1,0:T(8,128)(2,1)} copy(bf16[512,768]{0,1:T(8,128)(2,1)} %bitcast.119) | data formatting | bytes 1572864 | tf_op jit(solution)/shard_map/convert_element_type | solution.py:69
  (19 shorter events, 0.7 us)
Async XLA Ops:
  6.5 2.1 %copy-start = (bf16[768,2304]{1,0:T(8,128)(2,1)S(1)}, bf16[768,2304]{1,0:T(8,128)(2,1)}, u32[]{:S(2)}) copy-start(bf16[768,2304]{1,0:T(8,128)(2,1)} %param.7) | copy-start | bytes 10616836
  6.5 131.4 %all-reduce.2.cloned.1.call-start = ((), (), s32[]{:S(2)}) async-start(), calls=%async_computation | async-start | bytes 7077888 | tf_op jit(solution)/shard_map/psum | solution.py:55
  17.9 2.5 %copy-start.3 = (bf16[512,768]{0,1:T(8,128)(2,1)S(1)}, bf16[512,768]{0,1:T(8,128)(2,1)}, u32[]{:S(2)}) copy-start(bf16[512,768]{0,1:T(8,128)(2,1)} %copy.16) | copy-start | bytes 2359300
  17.9 2.5 %copy-start.6 = (f32[4,192,384]{2,1,0:T(8,128)S(1)}, f32[4,192,384]{2,1,0:T(8,128)}, u32[]{:S(2)}) copy-start(f32[4,192,384]{2,1,0:T(8,128)} %param.9) | copy-start | bytes 3538948
  20.4 1.1 copy-start.4
  20.4 1.5 copy-start.5
  138.0 3.1 %copy-start.2 = (f32[12,192,384]{2,1,0:T(8,128)S(1)}, f32[12,192,384]{2,1,0:T(8,128)}, u32[]{:S(2)}) copy-start(f32[12,192,384]{2,1,0:T(8,128)} %all-reduce.2.cloned.1.call-done) | copy-start | bytes 10616836
  141.5 1.2 copy-start.1
  188.7 2.3 %copy-start.7 = (bf16[512,768]{0,1:T(8,128)(2,1)S(1)}, bf16[512,768]{0,1:T(8,128)(2,1)}, u32[]{:S(2)}) copy-start(bf16[512,768]{0,1:T(8,128)(2,1)} %copy.18) | copy-start | bytes 2359300
  188.7 2.3 %copy-start.8 = (bf16[12,192,384]{2,1,0:T(8,128)(2,1)S(1)}, bf16[12,192,384]{2,1,0:T(8,128)(2,1)}, u32[]{:S(2)}) copy-start(bf16[12,192,384]{2,1,0:T(8,128)(2,1)} %fusion) | copy-start | bytes 5308420
Sparse Core Ops, SparseCore 0:
  29.0 108.8 all-reduce.1
where the time goes:
time: 203 us
  waiting for transfers between devices  107 us (53%)
  matrix products  62.4 us (31%)
  between operations  14.2 us (7%)
  local copies, waits for them, and re-layouts  11.6 us (6%)
  other arithmetic  7.94 us (4%)
    psum x1, waiting for transfers between devices, shards(): total = lax.psum(grads, 'tok')  107 us
    dot_general x5, matrix products, newton(): jnp.einsum('mij,mjk->mik', mixer, iterate, preferred_element_type=jnp.flo...  28.9 us
    dot_general x5, matrix products, newton(): jnp.einsum('mik,mjk->mij', iterate, iterate, preferred_element_type=jnp.f...  17.1 us
  transfers between devices with their start and end apart: 1, of which 1 were waited for; matrix products, arithmetic and copies ran while one was open for 1% of the time, Pallas kernels for 0%

commit v1 on v0

--- a/solution.py
+++ b/solution.py
@@ -52,7 +52,10 @@
     grad_up = jnp.einsum("thd,thf->hdf", keys, dup, preferred_element_type=jnp.float32)
     grad_down = -jnp.einsum("the,thf->hef", masked, hidden, preferred_element_type=jnp.float32)
     grads = jnp.concatenate([grad_gate, grad_up, grad_down], axis=0)
-    total = lax.psum(grads, "tok")
+    size, total = (lax.axis_size("tok"), grads)
+    for hop in [1 << k for k in range(size.bit_length() - 1)]:
+        route = [(i, i ^ hop) for i in range(size)]
+        total = total + lax.ppermute(total, "tok", route)
     norms = jnp.sqrt(jnp.sum(total * total, axis=(1, 2)))
     start = (total / (norms + 1e-07)[:, None, None]).astype(jnp.bfloat16)
     ortho = newton(start)

time: 203 us -> 375 us (1.85)
  waiting for transfers between devices: 107 us -> 308 us
  matrix products: 62.4 us -> 43.5 us
  between operations: 14.2 us -> 0.83 us
  starting transfers between devices: 0.01 us -> 7.9 us
  local copies, waits for them, and re-layouts: 11.6 us -> 6.74 us
    ppermute x0 -> x4, waiting for transfers between devices: none -> 308 us  [shards(): total = total + lax.ppermute(total, 'tok', route)]
    psum x1 -> x0, waiting for transfers between devices: 107 us -> none  [shards(): total = lax.psum(grads, 'tok')]
    dot_general x5, matrix products: 28.9 us -> 19.6 us  [newton(): jnp.einsum('mij,mjk->mik', mixer, iterate, preferred_element_type=jnp.flo...]
    dot_general x5, matrix products: 17.1 us -> 9.15 us  [newton(): jnp.einsum('mik,mjk->mij', iterate, iterate, preferred_element_type=jnp.f...]
    ppermute x0 -> x4, starting transfers between devices: none -> 7.9 us  [shards(): total = total + lax.ppermute(total, 'tok', route)]
  transfers between devices with their start and end apart: 1 -> 4, of which waited for: 1 -> 4; matrix products, arithmetic and copies ran while one was open for 1% -> 1% of each run, Pallas kernels for 0% -> 0%
where the time goes in v1:
time: 375 us; the launch traced here: 374 us
  waiting for transfers between devices  308 us (82%)
  matrix products  43.5 us (12%)
  starting transfers between devices  7.9 us (2%)
  other arithmetic  7.08 us (2%)
  local copies, waits for them, and re-layouts  6.74 us (2%)
    ppermute x4, waiting for transfers between devices, shards(): total = total + lax.ppermute(total, 'tok', route)  308 us
    dot_general x5, matrix products, newton(): jnp.einsum('mij,mjk->mik', mixer, iterate, preferred_element_type=jnp.flo...  19.6 us
    dot_general x5, matrix products, newton(): jnp.einsum('mik,mjk->mij', iterate, iterate, preferred_element_type=jnp.f...  9.15 us
    ppermute x4, starting transfers between devices, shards(): total = total + lax.ppermute(total, 'tok', route)  7.9 us
  transfers between devices with their start and end apart: 4, of which 4 were waited for; matrix products, arithmetic and copies ran while one was open for 1% of the time, Pallas kernels for 0%

profile of v1, /device:TPU:0, one launch (start us, length us, event | category | flops | bytes accessed | tf_op | source)
XLA Modules:
  0.0 374.2 jit_solution(4084092790220239935)
XLA Ops:
  0.0 1.4 fusion.40
  2.1 3.1 convolution_convert_fusion
  5.3 1.0 fusion.55
  7.6 0.8 fusion.34
  8.8 0.8 fusion.36
  10.1 0.8 fusion.38
  10.9 1.1 fusion.20
  12.1 1.9 fusion.18
  13.9 1.1 fusion.14
  15.9 5.8 %collective-permute-done = f32[12,192,384]{2,1,0:T(8,128)S(1)} collective-permute-done((f32[12,192,384]{2,1,0:T(8,128)S(1)}, f32[12,192,384]{2,1,0:T(8,128)S(1)}, u32[]{:S(2)}, u32[]{:S(2)}) %collective-permute-start) | collective-permute-done | bytes 3538976 | tf_op jit(solution)/shard_map/ppermute | solution.py:58
  22.2 3.0 collective-permute-start.1
  25.1 76.8 %collective-permute-done.1 = f32[12,192,384]{2,1,0:T(8,128)S(1)} collective-permute-done((f32[12,192,384]{2,1,0:T(8,128)S(1)}, f32[12,192,384]{2,1,0:T(8,128)S(1)}, u32[]{:S(2)}, u32[]{:S(2)}) %collective-permute-start.1) | collective-permute-done | bytes 3538976 | tf_op jit(solution)/shard_map/ppermute | solution.py:58
  102.5 1.9 collective-permute-start.2
  104.4 76.3 %collective-permute-done.2 = f32[12,192,384]{2,1,0:T(8,128)S(1)} collective-permute-done((f32[12,192,384]{2,1,0:T(8,128)S(1)}, f32[12,192,384]{2,1,0:T(8,128)S(1)}, u32[]{:S(2)}, u32[]{:S(2)}) %collective-permute-start.2) | collective-permute-done | bytes 3538976 | tf_op jit(solution)/shard_map/ppermute | solution.py:58
  181.0 2.6 collective-permute-start.3
  183.6 2.3 copy.18
  185.9 149.2 %collective-permute-done.3 = f32[12,192,384]{2,1,0:T(8,128)} collective-permute-done((f32[12,192,384]{2,1,0:T(8,128)S(1)}, f32[12,192,384]{2,1,0:T(8,128)}, u32[]{:S(2)}, u32[]{:S(2)}) %collective-permute-start.3) | collective-permute-done | bytes 3538976 | tf_op jit(solution)/shard_map/ppermute | solution.py:58
  335.1 2.5 multiply_reduce_fusion
  338.1 1.8 convolution_convert_fusion.5
  339.9 3.5 add_convert_fusion.4
  343.4 1.8 convolution_convert_fusion.4
  345.2 3.5 add_convert_fusion.3
  348.7 1.8 convolution_convert_fusion.3
  350.5 3.5 add_convert_fusion.2
  354.0 1.8 convolution_convert_fusion.2
  355.9 3.5 add_convert_fusion.1
  359.4 1.8 convolution_convert_fusion.1
  361.2 5.7 %fusion = bf16[12,192,384]{2,1,0:T(8,128)(2,1)} fusion(f32[4,192,384]{2,1,0:T(8,128)S(1)} %bitcast.116, f32[4,192,384]{2,1,0:T(8,128)} %param.9, f32[4,192,384]{2,1,0:T(8,128)} %param.8, bf16[12,192,384]{2,1,0:T(8,128)(2,1)S(1)} %add_convert_fusion.1, bf16[12,192,192]{2,1,0:T(8,128)(2,1)} %convolution_convert_fusion.1), kind=kOutput, calls=%fused_computation.2 | convolution fusion | flops 520667136 | bytes 7962624 | tf_op jit(solution)/shard_map/mij,mjk->mik/dot_general | solution.py:22
  366.9 2.3 fusion.56
  369.2 1.1 fusion.1
  370.3 1.6 convolution_convert_fusion.6
  371.9 2.3 copy.20
  (25 shorter events, 4.7 us)
Async XLA Ops:
  0.0 2.1 copy-start
  6.3 1.3 copy-start.5
  7.6 1.3 copy-start.4
  8.8 1.3 copy-start.2
  15.4 6.4 %collective-permute-start = (f32[12,192,384]{2,1,0:T(8,128)S(1)}, f32[12,192,384]{2,1,0:T(8,128)S(1)}, u32[]{:S(2)}, u32[]{:S(2)}) collective-permute-start(f32[12,192,384]{2,1,0:T(8,128)S(1)} %pad_maximum_fusion), channel_id=1, source_target_pairs={{0,1},{1,0},{2,3},{3,2},{4,5},{5,4},{6,7},{7,6},{8,9},{9,8},{10,11... | collective-permute-start | bytes 10616840 | tf_op jit(solution)/shard_map/ppermute | solution.py:58
  22.2 79.8 %collective-permute-start.1 = (f32[12,192,384]{2,1,0:T(8,128)S(1)}, f32[12,192,384]{2,1,0:T(8,128)S(1)}, u32[]{:S(2)}, u32[]{:S(2)}) collective-permute-start(f32[12,192,384]{2,1,0:T(8,128)S(1)} %fusion.54), channel_id=1, source_target_pairs={{0,2},{1,3},{2,0},{3,1},{4,6},{5,7},{6,4},{7,5},{8,10},{9,11},{10,... | collective-permute-start | bytes 10616840 | tf_op jit(solution)/shard_map/ppermute | solution.py:58
  102.5 78.1 %collective-permute-start.2 = (f32[12,192,384]{2,1,0:T(8,128)S(1)}, f32[12,192,384]{2,1,0:T(8,128)S(1)}, u32[]{:S(2)}, u32[]{:S(2)}) collective-permute-start(f32[12,192,384]{2,1,0:T(8,128)S(1)} %add.63), channel_id=1, source_target_pairs={{0,4},{1,5},{2,6},{3,7},{4,0},{5,1},{6,2},{7,3},{8,12},{9,13},{10,... | collective-permute-start | bytes 10616840 | tf_op jit(solution)/shard_map/ppermute | solution.py:58
  181.0 154.1 %collective-permute-start.3 = (f32[12,192,384]{2,1,0:T(8,128)S(1)}, f32[12,192,384]{2,1,0:T(8,128)}, u32[]{:S(2)}, u32[]{:S(2)}) collective-permute-start(f32[12,192,384]{2,1,0:T(8,128)S(1)} %add.64), channel_id=1, source_target_pairs={{0,8},{1,9},{2,10},{3,11},{4,12},{5,13},{6,14},{7,15},{8,0},{9,1},... | collective-permute-start | bytes 10616840 | tf_op jit(solution)/shard_map/ppermute | solution.py:58
  359.3 1.8 copy-start.3
  366.8 2.3 copy-start.6
  366.9 2.3 copy-start.7
  370.3 3.9 %copy-start.1 = (bf16[768,2304]{1,0:T(8,128)(2,1)S(1)}, bf16[768,2304]{1,0:T(8,128)(2,1)}, u32[]{:S(2)}) copy-start(bf16[768,2304]{1,0:T(8,128)(2,1)} %param.7) | copy-start | bytes 10616836
